TPU v7x, 32 devices: a whole 2x2x4 slice. The times are simulated.
32 devices in a mesh: pole: 2 (over y), row: 4 (over z), col: 4 (over x, core).
Axes of the slice: x: 2, y: 2, z: 4, core: 2. Of those that a mesh axis runs over, the one named last changes fastest.
Arguments:
- inverse_blocks: bfloat16 [128, 64, 128, 128], P(('pole', 'row'), 'col'), parts along dimension 0, may hold values from -6 to 6
- panel: bfloat16 [8, 32, 128, 128], P(('pole', 'row')), parts along dimension 0, may hold values from -0.09375 to 0.09375
- lists: int32 [4, 32], replicated, may hold values from 0 to 63, as said below
- diag_inverse: float32 [8, 128, 128], P(('pole', 'col')), parts along dimension 0, may hold values from -6 to 6
Outputs:
- offdiag: bfloat16 [8, 64, 128, 128], P(('pole', 'col'), 'row'), parts along dimension 0
- diagonal: float32 [8, 128, 128], P(('pole', 'col')), parts along dimension 0
There are 2 independent parts, one for each index of `pole`. A program takes and returns all parts, laid end to end along the dimension named above; an argument that names none is the same for every part. Nothing has to cross between parts.
Inputs may be any that keep to these rules, and one draw needn't show every extreme that they name: `lists`: each row holds 32 different ancestor block numbers in increasing order; at most 6 of them lie in any aligned group of 8 consecutive numbers, and every row has exactly 6 in some group.
All inputs are finite; a program needn't handle non-finite values.
Results may differ from a plain program's by a relative error of at most 0.0075.
Values may be sent and summed in bfloat16 or wider, within the bound.
A program may use at most 128 MiB of HBM per device.

v0:
```python
import jax
import jax.numpy as jnp
from jax import lax
from jax.sharding import PartitionSpec as P


def expand_blocks(blocks, rows, total):
    numbers = jnp.arange(total, dtype=jnp.int32)
    onehot = (rows[:, :, None] == numbers[None, None, :]).astype(jnp.bfloat16)
    spread = jnp.einsum("kln,klab->knab", onehot, blocks, preferred_element_type=jnp.float32)
    return spread.astype(jnp.bfloat16)


def per_device(inverse_blocks, panel, lists, diag_inverse):
    n_row = lax.axis_size("row")
    n_col = lax.axis_size("col")
    k_local, n_list, width = (panel.shape[0], panel.shape[1], panel.shape[2])
    rows_here, cols_here = (inverse_blocks.shape[0], inverse_blocks.shape[1])
    total = rows_here * n_row
    n_super = k_local * n_row
    k_col = n_super // n_col
    row_index = lax.axis_index("row")
    col_index = lax.axis_index("col")
    col_base = col_index * cols_here
    owned = lax.dynamic_slice_in_dim(lists, row_index * k_local, k_local, 0)
    expanded = expand_blocks(panel, owned, total)
    outgoing = expanded.reshape(k_local, n_row, rows_here, width, width)
    incoming = lax.all_to_all(outgoing, "row", split_axis=1, concat_axis=0, tiled=True)
    row_panel = incoming.reshape(n_super, rows_here, width, width)
    group_width = total // 8
    slot_count = 6
    group_count = total // group_width
    groups_here = cols_here // group_width
    first_group = col_index * groups_here
    bounds = jnp.arange(group_count, dtype=jnp.int32) * group_width
    starts_all = jnp.sum((lists[:, None, :] < bounds[None, :, None]).astype(jnp.int32), axis=2)
    ends_all = jnp.concatenate(
        [starts_all[:, 1:], jnp.full((n_super, 1), n_list, jnp.int32)], axis=1
    )
    counts_all = ends_all - starts_all
    my_starts = lax.dynamic_slice(
        starts_all, (row_index * k_local, first_group), (k_local, groups_here)
    )
    padded = jnp.concatenate(
        [panel, jnp.zeros((k_local, slot_count, width, width), panel.dtype)], axis=1
    )

    def take_slots(blocks, begin):
        return lax.dynamic_slice_in_dim(blocks, begin, slot_count, 0)

    def take_groups(blocks, begins):
        return jax.vmap(lambda begin: take_slots(blocks, begin))(begins)

    packed = jax.vmap(take_groups)(padded, my_starts)
    packed = packed.reshape(k_local, groups_here * slot_count, width, width)
    block_starts = lax.dynamic_slice_in_dim(starts_all, first_group, groups_here, 1)
    block_counts = lax.dynamic_slice_in_dim(counts_all, first_group, groups_here, 1)
    slots = jnp.arange(slot_count, dtype=jnp.int32)
    position = jnp.minimum(block_starts[:, :, None] + slots[None, None, :], n_list - 1)
    named = (
        jnp.take_along_axis(lists, position.reshape(n_super, groups_here * slot_count), axis=1)
        - col_base
    )
    valid = (slots[None, None, :] < block_counts[:, :, None]).reshape(
        n_super, groups_here * slot_count
    )
    target = jnp.where(valid, named, -1)
    columns = jnp.arange(cols_here, dtype=jnp.int32)
    onehot = (target[:, :, None] == columns[None, None, :]).astype(jnp.bfloat16)
    spread = jnp.einsum(
        "msj,msab->mjab",
        onehot,
        lax.all_gather(packed, "row", axis=0, tiled=True),
        preferred_element_type=jnp.float32,
    )
    partial_sum = jnp.einsum(
        "ijab,mjbc->miac",
        inverse_blocks,
        spread.astype(jnp.bfloat16),
        preferred_element_type=jnp.float32,
    )
    summed = lax.psum_scatter(partial_sum, "col", scatter_dimension=0, tiled=True)
    chosen_rows = lax.dynamic_slice_in_dim(row_panel, col_index * k_col, k_col, 0)
    local_quad = jnp.einsum(
        "kiab,kiac->kbc", chosen_rows.astype(jnp.float32), summed, precision=lax.Precision.HIGHEST
    )
    quad = lax.psum(local_quad.astype(jnp.bfloat16), "row").astype(jnp.float32)
    diagonal = diag_inverse + quad
    keep_rows = row_index * rows_here + jnp.arange(rows_here, dtype=jnp.int32)
    owned_col = lax.dynamic_slice_in_dim(lists, col_index * k_col, k_col, 0)
    present = jnp.any(owned_col[:, :, None] == keep_rows[None, None, :], axis=1).astype(jnp.float32)
    offdiag = (-summed * present[:, :, None, None]).astype(jnp.bfloat16)
    return (offdiag, diagonal)


def solution(mesh):
    in_specs = (
        P(("pole", "row"), "col", None, None),
        P(("pole", "row"), None, None, None),
        P(),
        P(("pole", "col"), None, None),
    )
    out_specs = (P(("pole", "col"), "row", None, None), P(("pole", "col"), None, None))
    return jax.shard_map(
        per_device, mesh=mesh, in_specs=in_specs, out_specs=out_specs, check_vma=False
    )
```

profile of v0, /device:TPU:0, one launch (start us, length us, event | category | flops | bytes accessed | tf_op | source)
XLA Modules:
  0.0 146.1 jit_solution(12334185304761213798)
XLA Ops:
  7.2 0.0 copy-start
  7.2 0.0 all-gather.2.cloned.1.call-start
  7.2 0.9 convert_reduce_fusion
  8.1 0.1 fusion.31
  8.2 0.1 copy.41
  8.3 0.1 pad_bitcast_fusion
  8.4 0.2 or_reduce_fusion
  8.6 1.4 concatenate.10
  10.0 1.3 gather_fusion.1
  11.3 0.0 all-gather.2.cloned.1.call-update
  11.3 0.0 reduce-scatter.2.cloned.1.call-start
  11.4 0.1 slice.3
  11.5 0.1 constant_dynamic-slice_fusion.3
  11.5 0.1 add.94
  11.6 0.1 add.99
  11.7 0.1 add.95
  11.8 0.1 lt.90
  11.9 0.1 reshape.275
  12.0 0.0 copy-done
  12.0 1.1 gather_fusion
  13.0 0.1 reshape.278
  13.1 0.1 lt.96
  13.2 0.1 lt.97
  13.3 12.7 %copy.30 = bf16[16,16,128,128]{2,1,3,0:T(8,128)(2,1)} copy(bf16[16,16,128,128]{3,2,1,0:T(8,128)(2,1)} %param.4) | data formatting | bytes 16777216 | tf_op args[0]
  26.0 25.3 %all-gather.2.cloned.1.call-done = bf16[4,12,128,128]{3,2,1,0:T(8,128)(2,1)} async-done(((bf16[1,12,128,128]{3,2,1,0:T(8,128)(2,1)}), bf16[4,12,128,128]{3,2,1,0:T(8,128)(2,1)}) %all-gather.2.cloned.1.call-update) | async-done | bytes 1572880 | tf_op jit(solution)/shard_map/all_gather | solution.py:73
  51.3 10.6 %fusion.2 = f32[4,16,128,128]{2,3,1,0:T(8,128)} fusion(bf16[16,16,128,128]{2,1,3,0:T(8,128)(2,1)} %copy.30, bf16[4,12,128,128]{3,2,1,0:T(8,128)(2,1)} %all-gather.2.cloned.1.call-done, s32[4,12]{1,0:T(4,128)S(1)} %subtract_select_fusion), kind=kOutput, calls=%fused_computation.4 | convolution fusion | flops 4321182720 | bytes 14155968 | tf_op jit(solution)/shard_map/ijab,mjbc->miac/dot_general | solution.py:76
  61.9 0.0 copy-start.1
  61.9 0.0 reduce-scatter.2.cloned.1.call-update
  61.9 1.2 copy-done.1
  63.1 1.0 convolution_convert_fusion
  64.1 1.7 %copy.32 = bf16[1,4,16,128,128]{4,2,3,0,1:T(8,128)(2,1)} copy(bf16[1,4,16,128,128]{4,2,1,3,0:T(8,128)(2,1)S(1)} %bitcast.54) | data formatting | bytes 4194304 | tf_op jit(solution)/shard_map/reshape | solution.py:27
  65.8 3.6 %all-to-all-start = ((bf16[1,4,16,128,128]{4,2,3,0,1:T(8,128)(2,1)}), bf16[1,4,16,128,128]{4,2,3,0,1:T(8,128)(2,1)S(1)}, u32[]{:S(2)}, u32[]{:S(2)}) async-start(bf16[1,4,16,128,128]{4,2,3,0,1:T(8,128)(2,1)} %copy.32), calls=%async_computation.1 | async-start | bytes 4194304 | tf_op jit(solution)/shard_map/all_to_all | solution.py:28
  69.5 0.2 compare_reduce_fusion
  69.7 48.1 %all-to-all-done = bf16[1,4,16,128,128]{4,2,3,0,1:T(8,128)(2,1)S(1)} async-done(((bf16[1,4,16,128,128]{4,2,3,0,1:T(8,128)(2,1)}), bf16[1,4,16,128,128]{4,2,3,0,1:T(8,128)(2,1)S(1)}, u32[]{:S(2)}, u32[]{:S(2)}) %all-to-all-start) | async-done | bytes 2097184 | tf_op jit(solution)/shard_map/all_to_all | solution.py:28
  117.8 0.5 copy.33
  118.3 0.0 copy-start.3
  118.3 0.0 reduce-scatter.2.cloned.1.call-done
  118.3 0.0 copy-start.2
  118.3 2.0 %fusion.14 = bf16[1,128,128]{2,1,0:T(8,128)(2,1)S(1)} fusion(f32[1,16,128,128]{2,3,1,0:T(8,128)} %reduce-scatter.2.cloned.1.call-done, bf16[1,1,16,128,128]{3,4,2,1,0:T(8,128)(2,1)S(1)} %copy.33), kind=kOutput, calls=%fused_computation.12 | convolution fusion | flops 402669568 | bytes 1605632 | tf_op jit(solution)/shard_map/kiab,kiac->kbc/dot_general | solution.py:84
  120.3 17.1 %psum.7 = bf16[1,128,128]{2,1,0:T(8,128)(2,1)S(1)} all-reduce(bf16[1,128,128]{2,1,0:T(8,128)(2,1)S(1)} %fusion.14), channel_id=1, replica_groups=mesh['pole'=2,'row'=4,'col'=4] {'row'}, use_global_device_ids=true, to_apply=%region_3.4 | all-reduce | flops 16384 | bytes 65536 | tf_op jit(solution)/shard_map/psum | solution.py:87
  137.4 0.0 copy-done.2
  137.4 0.2 multiply_convert_fusion
  137.6 1.0 copy.35
  138.6 0.0 copy-done.3
  138.6 0.6 convert_add_fusion
  (9 shorter events, 0.1 us)
Async XLA Ops:
  7.2 4.8 %copy-start = (s32[4,32]{1,0:T(4,128)S(1)}, s32[4,32]{1,0:T(4,128)}, u32[]{:S(2)}) copy-start(s32[4,32]{1,0:T(4,128)} %param.6) | copy-start | bytes 1540
  7.2 44.1 %all-gather.2.cloned.1.call-start = ((), (), s32[]{:S(2)}) async-start(), calls=%async_computation.2 | async-start | bytes 1966080 | tf_op jit(solution)/shard_map/all_gather | solution.py:73
  11.3 107.0 %reduce-scatter.2.cloned.1.call-start = ((), (), s32[]{:S(2)}) async-start(), calls=%async_computation.3 | async-start | bytes 5242880 | tf_op jit(solution)/shard_map/reduce_scatter | solution.py:82
  61.9 1.2 copy-start.1
  65.8 51.9 %all-to-all-start = ((bf16[1,4,16,128,128]{4,2,3,0,1:T(8,128)(2,1)}), bf16[1,4,16,128,128]{4,2,3,0,1:T(8,128)(2,1)S(1)}, u32[]{:S(2)}, u32[]{:S(2)}) async-start(bf16[1,4,16,128,128]{4,2,3,0,1:T(8,128)(2,1)} %copy.32), calls=%async_computation.1 | async-start | bytes 4194304 | tf_op jit(solution)/shard_map/all_to_all | solution.py:28
  118.3 20.4 %copy-start.3 = (f32[1,128,128]{2,1,0:T(8,128)S(1)}, f32[1,128,128]{2,1,0:T(8,128)}, u32[]{:S(2)}) copy-start(f32[1,128,128]{2,1,0:T(8,128)} %param.7) | copy-start | bytes 196612
  118.3 19.1 %copy-start.2 = (f32[1,16,128,128]{2,3,1,0:T(8,128)S(1)}, f32[1,16,128,128]{2,3,1,0:T(8,128)}, u32[]{:S(2)}) copy-start(f32[1,16,128,128]{2,3,1,0:T(8,128)} %reduce-scatter.2.cloned.1.call-done) | copy-start | bytes 3145732
Sparse Core Ops, SparseCore 0:
  11.4 39.7 all-gather.1
  62.0 43.3 reduce-scatter.1
where the time goes:
time: 147 us; the launch traced here: 146 us
  waiting for transfers between devices  73.4 us (50%)
  local copies, waits for them, and re-layouts  21.9 us (15%)
  blocking collectives  17.1 us (12%)
  between operations  14.2 us (10%)
  matrix products  13.6 us (9%)
  starting transfers between devices  3.73 us (3%)
  other arithmetic  2.2 us (1%)
    all_to_all x1, waiting for transfers between devices, per_device(): lax.all_to_all(outgoing, 'row', split_axis=1, concat_axis=0, tiled=True)  48.1 us
    all_gather x1, waiting for transfers between devices, per_device(): lax.all_gather(packed, 'row', axis=0, tiled=True)  25.3 us
    psum x1, blocking collectives, per_device(): quad = lax.psum(local_quad.astype(jnp.bfloat16), 'row').astype(jnp.float32)  17.1 us
    unnamed x11, local copies, waits for them, and re-layouts  15 us
    dot_general x1, matrix products, per_device(): jnp.einsum('ijab,mjbc->miac', inverse_blocks, spread.astype(jnp.bfloat16)...  10.6 us
    all_to_all x1, starting transfers between devices, per_device(): lax.all_to_all(outgoing, 'row', split_axis=1, concat_axis=0, tiled=True)  3.65 us
  transfers between devices with their start and end apart: 3, of which 2 were waited for; matrix products, arithmetic and copies ran while one was open for 12% of the time, Pallas kernels for 0%

commit v1 on v0

v1 whole, which is shorter than its diff:
```python
import functools

import jax
import jax.numpy as jnp
from jax import lax
from jax.experimental import pallas as pl
from jax.experimental.pallas import tpu as pltpu
from jax.sharding import PartitionSpec as P

GROUP = 8
MOST = 6
MESH = pl.DeviceIdType.MESH


def slot_count(width, n_list):
    if width % GROUP == 0:
        count = width // GROUP * MOST
    elif GROUP % width == 0:
        count = min(width, MOST)
    else:
        count = width
    return min(count, n_list)


def kernel(
    n_row, n_col, k_col, rows_here, cols_here, n_list, slots_r, slots_c,
    lists, inv_hbm, panel_hbm, dinv, off, diag,
    inv, panel, got, cur, xs, part, acc, stage, x_stage, sib_in, dest_sib, dest_x,
    quadx, tot, quad_in,
    load_sem, up_s, down_s, x_r, qx_s, qx_r, st_s, sib_r, dsib_r, xs_s, dx_r, q_s, q_r,
):
    r = lax.axis_index("row")
    c = lax.axis_index("col")
    width = inv.shape[-1]
    chip, core = c // 2, c % 2
    sibling = chip * 2 + 1 - core
    half = slots_r // 2
    n_chip = n_col // 2
    row_base, col_base = r * rows_here, c * cols_here
    c_src = row_base // cols_here

    load_panel = pltpu.make_async_copy(panel_hbm.at[0], panel, load_sem.at[0])
    load_inv = pltpu.make_async_copy(inv_hbm, inv, load_sem.at[1])
    load_panel.start()
    load_inv.start()

    barrier = pltpu.get_barrier_semaphore()
    for step in range(1, n_row):
        pl.semaphore_signal(barrier, inc=1, device_id={"row": lax.rem(r + step, n_row)}, device_id_type=MESH)
    for step in range(1, n_col):
        pl.semaphore_signal(barrier, inc=1, device_id={"col": lax.rem(c + step, n_col)}, device_id_type=MESH)

    def before(k, bound):
        total = jnp.int32(0)
        for l in range(n_list):
            total += jnp.where(lists[k, l] < bound, 1, 0).astype(jnp.int32)
        return total

    def first(begin, slots):
        return jnp.minimum(begin, n_list - slots)

    cur[slots_c] = jnp.zeros((width, width), cur.dtype)
    tot[slots_r] = jnp.zeros((width, width), tot.dtype)
    mine = first(before(r, col_base), slots_c)
    load_panel.wait()
    got[r] = panel[pl.ds(mine, slots_c)]
    pl.semaphore_wait(barrier, n_row + n_col - 2)

    def go_up(k):
        return pltpu.make_async_remote_copy(
            got.at[k], got.at[k], up_s.at[k], x_r.at[k], device_id={"row": r + 1}, device_id_type=MESH)

    def go_down(k):
        return pltpu.make_async_remote_copy(
            got.at[k], got.at[k], down_s.at[k], x_r.at[k], device_id={"row": r - 1}, device_id_type=MESH)

    def send_rows(k):
        return pltpu.make_async_remote_copy(
            got.at[k], quadx.at[k % k_col], qx_s.at[k], qx_r.at[k % k_col],
            device_id={"col": k // k_col}, device_id_type=MESH)

    def send_to_owner(k, h):
        return pltpu.make_async_remote_copy(
            stage.at[k, h], dest_sib.at[k % k_col, h], st_s.at[k, h], dsib_r.at[k % k_col, h],
            device_id={"col": k // k_col}, device_id_type=MESH)

    def send_to_sibling(k, h):
        return pltpu.make_async_remote_copy(
            stage.at[k, h], sib_in.at[k], st_s.at[k, h], sib_r.at[k],
            device_id={"col": sibling}, device_id_type=MESH)

    def send_across(k):
        return pltpu.make_async_remote_copy(
            x_stage.at[k], dest_x.at[k % k_col, chip, core], xs_s.at[k],
            dx_r.at[k % k_col, chip, core],
            device_id={"col": k // k_col}, device_id_type=MESH)

    def use(k):
        owner = k // k_col
        at = k % k_col

        @pl.when(k != r)
        def _():
            go_up(k).wait_recv()

        @pl.when((k <= r) & (r < n_row - 1))
        def _():
            go_up(k).start()

        @pl.when((k >= r) & (r > 0))
        def _():
            go_down(k).start()

        @pl.when((c == c_src) & (owner == c))
        def _():
            quadx[at] = got[k]

        @pl.when((c == c_src) & (owner != c))
        def _():
            send_rows(k).start()

        begin = before(k, col_base)
        base = first(begin, slots_c)
        cur[0:slots_c] = got[k]
        p = begin
        for j in range(cols_here):
            hit = lists[k, jnp.minimum(p, n_list - 1)] == col_base + j
            slot = jnp.where(hit, jnp.clip(p - base, 0, slots_c - 1), slots_c)
            xs[j * width : (j + 1) * width, :] = cur[slot]
            p += hit.astype(jnp.int32)

        @pl.when(k == r)
        def _():
            load_inv.wait()

        row_first = first(before(k, row_base), slots_r)

        def half_step(turn, carry):
            h = (core + 1 + turn) % 2
            lines = []
            for s in range(half):
                i = jnp.clip(lists[k, row_first + h * half + s] - row_base, 0, rows_here - 1)
                blocks = inv[i]
                lines.append(jnp.concatenate([blocks[j] for j in range(cols_here)], axis=1))
            left = jnp.concatenate(lines, axis=0)
            part[...] = jnp.dot(left, xs[...], preferred_element_type=jnp.float32)

            @pl.when(owner == c)
            def _():
                acc[at, h] = part[...]

            @pl.when(owner == sibling)
            def _():
                stage[k, h] = part[...].astype(stage.dtype)
                send_to_owner(k, h).start()

            @pl.when((owner // 2 != chip) & (turn == 0))
            def _():
                stage[k, h] = part[...].astype(stage.dtype)
                send_to_sibling(k, h).start()

            @pl.when((owner // 2 != chip) & (turn == 1))
            def _():
                send_to_sibling(k, h).wait_recv()
                x_stage[k] = (part[...] + sib_in[k].astype(jnp.float32)).astype(x_stage.dtype)
                send_across(k).start()

            return carry

        lax.fori_loop(0, 2, half_step, 0)

    def turn_step(t, carry):
        s = (t + 1) // 2
        k = r + jnp.where(t % 2 == 1, -s, s)

        @pl.when((k >= 0) & (k < n_row))
        def _():
            use(k)

        return carry

    lax.fori_loop(0, 2 * n_row - 1, turn_step, 0)

    def finish(at, carry):
        k = c * k_col + at

        @pl.when(c != c_src)
        def _():
            send_rows(k).wait_recv()

        for h in range(2):
            send_to_owner(k, h).wait_recv()
        total = acc[at].astype(jnp.float32) + dest_sib[at].astype(jnp.float32)
        tot[0:slots_r] = total.reshape(slots_r, width, width)
        for step in range(1, n_chip):
            other = lax.rem(chip + step, n_chip)
            for h in range(2):
                pltpu.make_async_remote_copy(
                    x_stage.at[k], dest_x.at[at, other, h], xs_s.at[k], dx_r.at[at, other, h],
                    device_id={"col": other * 2 + h}, device_id_type=MESH).wait_recv()
            come = dest_x[at, other].astype(jnp.float32)
            tot[0:slots_r] = tot[0:slots_r] + come.reshape(slots_r, width, width)

        begin = before(k, row_base)
        row_first = first(begin, slots_r)
        p = begin
        for i in range(rows_here):
            hit = lists[k, jnp.minimum(p, n_list - 1)] == row_base + i
            slot = jnp.where(hit, jnp.clip(p - row_first, 0, slots_r - 1), slots_r)
            off[at, i] = (-tot[slot]).astype(off.dtype)
            p += hit.astype(jnp.int32)

        col_first = first(before(k, c_src * cols_here), slots_c)
        cur[0:slots_c] = quadx[at]
        lines = []
        for s in range(slots_r):
            position = row_first + s
            number = lists[k, position] - row_base
            valid = (number >= 0) & (number < rows_here)
            slot = jnp.where(valid, jnp.clip(position - col_first, 0, slots_c - 1), slots_c)
            lines.append(cur[slot])
        left = jnp.concatenate(lines, axis=0)
        right = tot[0:slots_r].reshape(slots_r * width, width)
        high = right.astype(jnp.bfloat16)
        low = (right - high.astype(jnp.float32)).astype(jnp.bfloat16)
        both = lax.dot_general(
            left, jnp.concatenate([high, low], axis=1), (((0,), (0,)), ((), ())),
            preferred_element_type=jnp.float32)
        quad_in[r, at] = (both[:, :width] + both[:, width:]).astype(quad_in.dtype)
        return carry

    lax.fori_loop(0, k_col, finish, 0)

    def share(other):
        return pltpu.make_async_remote_copy(
            quad_in.at[r], quad_in.at[r], q_s.at[other], q_r.at[r],
            device_id={"row": other}, device_id_type=MESH)

    def take(other):
        return pltpu.make_async_remote_copy(
            quad_in.at[other], quad_in.at[other], q_s.at[other], q_r.at[other],
            device_id={"row": other}, device_id_type=MESH)

    def start_share(step, carry):
        share(lax.rem(r + step, n_row)).start()
        return carry

    lax.fori_loop(1, n_row, start_share, 0)

    def drain(k, carry):
        owner = k // k_col

        @pl.when((k <= r) & (r < n_row - 1))
        def _():
            go_up(k).wait_send()

        @pl.when((k >= r) & (r > 0))
        def _():
            go_down(k).wait_send()

        @pl.when((c == c_src) & (owner != c))
        def _():
            send_rows(k).wait_send()

        @pl.when(owner == sibling)
        def _():
            send_to_owner(k, 0).wait_send()
            send_to_owner(k, 1).wait_send()

        @pl.when(owner // 2 != chip)
        def _():
            send_to_sibling(k, 1 - core).wait_send()
            send_across(k).wait_send()

        return carry

    lax.fori_loop(0, n_row, drain, 0)

    def wait_share(step, carry):
        other = lax.rem(r + step, n_row)
        take(other).wait_recv()
        share(other).wait_send()
        return carry

    lax.fori_loop(1, n_row, wait_share, 0)

    quad = quad_in[0].astype(jnp.float32)
    for other in range(1, n_row):
        quad = quad + quad_in[other].astype(jnp.float32)
    diag[...] = dinv[...] + quad


def per_device(n_row, n_col, inverse_blocks, panel, lists, diag_inverse):
    rows_here, cols_here, width, _ = inverse_blocks.shape
    n_list = panel.shape[1]
    k_col = diag_inverse.shape[0]
    slots_r = slot_count(rows_here, n_list)
    slots_c = slot_count(cols_here, n_list)
    half = slots_r // 2
    n_super = n_row
    low, full = inverse_blocks.dtype, jnp.float32
    part = (half * width, width)
    dma = pltpu.SemaphoreType.DMA
    vmem = pl.BlockSpec(memory_space=pltpu.VMEM)
    return pl.pallas_call(
        functools.partial(
            kernel, n_row, n_col, k_col, rows_here, cols_here, n_list, slots_r, slots_c),
        out_shape=(
            jax.ShapeDtypeStruct((k_col, rows_here, width, width), low),
            jax.ShapeDtypeStruct((k_col, width, width), full),
        ),
        in_specs=[
            pl.BlockSpec(memory_space=pltpu.SMEM),
            pl.BlockSpec(memory_space=pl.ANY),
            pl.BlockSpec(memory_space=pl.ANY),
            vmem,
        ],
        out_specs=(vmem, vmem),
        scratch_shapes=[
            pltpu.VMEM(inverse_blocks.shape, low),
            pltpu.VMEM(panel.shape[1:], low),
            pltpu.VMEM((n_super, slots_c, width, width), low),
            pltpu.VMEM((slots_c + 1, width, width), low),
            pltpu.VMEM((cols_here * width, width), low),
            pltpu.VMEM(part, full),
            pltpu.VMEM((k_col, 2) + part, full),
            pltpu.VMEM((n_super, 2) + part, low),
            pltpu.VMEM((n_super,) + part, low),
            pltpu.VMEM((n_super,) + part, low),
            pltpu.VMEM((k_col, 2) + part, low),
            pltpu.VMEM((k_col, n_col // 2, 2) + part, low),
            pltpu.VMEM((k_col, slots_c, width, width), low),
            pltpu.VMEM((slots_r + 1, width, width), full),
            pltpu.VMEM((n_row, k_col, width, width), low),
            dma((2,)),
            dma((n_super,)),
            dma((n_super,)),
            dma((n_super,)),
            dma((n_super,)),
            dma((k_col,)),
            dma((n_super, 2)),
            dma((n_super,)),
            dma((k_col, 2)),
            dma((n_super,)),
            dma((k_col, n_col // 2, 2)),
            dma((n_row,)),
            dma((n_row,)),
        ],
        compiler_params=pltpu.CompilerParams(
            collective_id=0, has_side_effects=True, vmem_limit_bytes=50 * 1024 * 1024),
        name="selected_inverse",
    )(lists, inverse_blocks, panel, diag_inverse)


def solution(mesh):
    in_specs = (
        P(("pole", "row"), "col", None, None),
        P(("pole", "row"), None, None, None),
        P(),
        P(("pole", "col"), None, None),
    )
    out_specs = (P(("pole", "col"), "row", None, None), P(("pole", "col"), None, None))
    return jax.shard_map(
        functools.partial(per_device, mesh.shape["row"], mesh.shape["col"]),
        mesh=mesh, in_specs=in_specs, out_specs=out_specs, check_vma=False)
```

time: 147 us -> 53.4 us (0.36)
  waiting for transfers between devices: 73.4 us -> 0 us
  Pallas kernels: 0 us -> 48 us
  local copies, waits for them, and re-layouts: 21.9 us -> 4.16 us
  blocking collectives: 17.1 us -> 0 us
  matrix products: 13.6 us -> 0 us
  between operations: 14.2 us -> 0.65 us
  starting transfers between devices: 3.73 us -> 0 us
  other arithmetic: 2.2 us -> 0 us
    all_to_all x1 -> x0, waiting for transfers between devices: 48.1 us -> none  [per_device(): lax.all_to_all(outgoing, 'row', split_axis=1, concat_axis=0, tiled=True)]
    pallas_call x0 -> x1, Pallas kernels: none -> 48 us  [per_device(): pl.pallas_call(functools.partial(kernel, n_row, n_col, k_col, rows_here,...]
    all_gather x1 -> x0, waiting for transfers between devices: 25.3 us -> none  [per_device(): lax.all_gather(packed, 'row', axis=0, tiled=True)]
    psum x1 -> x0, blocking collectives: 17.1 us -> none  [per_device(): quad = lax.psum(local_quad.astype(jnp.bfloat16), 'row').astype(jnp.float32)]
    dot_general x3 -> x0, matrix products: 13.6 us -> none  [the longest x1 10.6 us: per_device(): jnp.einsum('ijab,mjbc->miac', inverse_blocks, spread.astype(jnp.bfloat16)...]
    unnamed x11 -> x8, local copies, waits for them, and re-layouts: 15 us -> 4.16 us
    all_to_all x1 -> x0, starting transfers between devices: 3.65 us -> none  [per_device(): lax.all_to_all(outgoing, 'row', split_axis=1, concat_axis=0, tiled=True)]
    gather x5 -> x0, local copies, waits for them, and re-layouts: 2.66 us -> none  [the longest x2 1.42 us: take_slots(): return lax.dynamic_slice_in_dim(blocks, begin, slot_count, 0)]
  transfers between devices with their start and end apart: 3 -> 0, of which waited for: 2 -> 0; matrix products, arithmetic and copies ran while one was open for 12% -> 0% of each run, Pallas kernels for 0% -> 0%
where the time goes in v1:
time: 53.4 us; the launch traced here: 52.8 us
  Pallas kernels  48 us (90%)
  local copies, waits for them, and re-layouts  4.16 us (8%)
  between operations  0.65 us (1%)
    pallas_call x1, Pallas kernels, per_device(): pl.pallas_call(functools.partial(kernel, n_row, n_col, k_col, rows_here,...  48 us
    unnamed x8, local copies, waits for them, and re-layouts  4.16 us

profile of v1, /device:TPU:0, one launch (start us, length us, event | category | flops | bytes accessed | tf_op | source)
XLA Modules:
  0.0 52.8 jit_solution(9598553318834365398)
XLA Ops:
  0.6 0.0 copy-start
  0.6 1.2 %copy-done = bf16[1,32,128,128]{3,2,1,0:T(8,128)(2,1)S(1)} copy-done((bf16[1,32,128,128]{3,2,1,0:T(8,128)(2,1)S(1)}, bf16[1,32,128,128]{3,2,1,0:T(8,128)(2,1)}, u32[]{:S(2)}) %copy-start) | copy-done | bytes 1048600
  1.9 0.0 copy-start.1
  1.9 0.8 %copy-done.1 = f32[1,128,128]{2,1,0:T(8,128)S(1)} copy-done((f32[1,128,128]{2,1,0:T(8,128)S(1)}, f32[1,128,128]{2,1,0:T(8,128)}, u32[]{:S(2)}) %copy-start.1) | copy-done | bytes 65560
  2.7 0.0 copy-start.2
  2.7 0.7 %copy-done.2 = s32[4,32]{1,0:T(4,128)S(1)} copy-done((s32[4,32]{1,0:T(4,128)S(1)}, s32[4,32]{1,0:T(4,128)}, u32[]{:S(2)}) %copy-start.2) | copy-done | bytes 536
  3.4 48.0 %selected_inverse.1 = (bf16[1,16,128,128]{3,2,1,0:T(8,128)(2,1)S(1)}, f32[1,128,128]{2,1,0:T(8,128)S(1)}) custom-call(s32[4,32]{1,0:T(4,128)S(1)} %copy-done.2, bf16[16,16,128,128]{3,2,1,0:T(8,128)(2,1)} %inv_hbm.1, bf16[1,32,128,128]{3,2,1,0:T(8,128)(2,1)S(1)} %copy-done, f32[1,128,128]{2,1,0:T(8,128)S(1)} %copy-done.1), custom_call_target="tpu_custom_call" | custom-call | tf_op jit(solution)/shard_map/selected_inverse/pallas_call | solution.py:305
  51.3 0.8 %copy.8 = bf16[1,16,128,128]{3,2,1,0:T(8,128)(2,1)} copy(bf16[1,16,128,128]{3,2,1,0:T(8,128)(2,1)S(1)} %get-tuple-element.4) | data formatting | bytes 1048576
  52.1 0.6 %copy.9 = f32[1,128,128]{2,1,0:T(8,128)} copy(f32[1,128,128]{2,1,0:T(8,128)S(1)} %get-tuple-element.5) | data formatting | bytes 131072
Async XLA Ops:
  0.6 1.2 %copy-start = (bf16[1,32,128,128]{3,2,1,0:T(8,128)(2,1)S(1)}, bf16[1,32,128,128]{3,2,1,0:T(8,128)(2,1)}, u32[]{:S(2)}) copy-start(bf16[1,32,128,128]{3,2,1,0:T(8,128)(2,1)} %panel_hbm.1) | copy-start | bytes 3145732
  1.9 0.8 %copy-start.1 = (f32[1,128,128]{2,1,0:T(8,128)S(1)}, f32[1,128,128]{2,1,0:T(8,128)}, u32[]{:S(2)}) copy-start(f32[1,128,128]{2,1,0:T(8,128)} %dinv.1) | copy-start | bytes 196612
  2.7 0.7 %copy-start.2 = (s32[4,32]{1,0:T(4,128)S(1)}, s32[4,32]{1,0:T(4,128)}, u32[]{:S(2)}) copy-start(s32[4,32]{1,0:T(4,128)} %lists.1) | copy-start | bytes 1540

commit v2 on v1

v2 whole, which is shorter than its diff:
```python
import functools

import jax
import jax.numpy as jnp
from jax import lax
from jax.experimental import pallas as pl
from jax.experimental.pallas import tpu as pltpu
from jax.sharding import PartitionSpec as P

GROUP = 8
MOST = 6
CHUNKS = 2
MESH = pl.DeviceIdType.MESH


def slot_count(width, n_list):
    if width % GROUP == 0:
        count = width // GROUP * MOST
    elif GROUP % width == 0:
        count = min(width, MOST)
    else:
        count = width
    return min(count, n_list)


def kernel(
    n_row, n_col, k_col, rows_here, cols_here, n_list, slots_r, slots_c,
    lists, inv_hbm, panel_hbm, dinv, off, diag,
    inv, panel, got, cur, xs, part, acc, stage, x_stage, sib_in, dest_x,
    quadx, tot, quad_out, quad_in,
    load_sem, up_s, down_s, x_r, qx_s, qx_r, st_s, sib_r, xs_s, dx_r, q_s, q_r,
):
    r = lax.axis_index("row")
    c = lax.axis_index("col")
    width = inv.shape[-1]
    chip, core = c // 2, c % 2
    sibling = chip * 2 + 1 - core
    half = slots_r // 2
    n_chip = n_col // 2
    row_base, col_base = r * rows_here, c * cols_here
    c_src = row_base // cols_here

    load_panel = pltpu.make_async_copy(panel_hbm.at[0], panel, load_sem.at[0])
    load_inv = pltpu.make_async_copy(inv_hbm, inv, load_sem.at[1])
    load_panel.start()
    load_inv.start()

    barrier = pltpu.get_barrier_semaphore()
    def greet(at, carry):
        @pl.when((at // n_col != r) | (at % n_col != c))
        def _():
            pl.semaphore_signal(
                barrier, inc=1, device_id={"row": at // n_col, "col": at % n_col}, device_id_type=MESH)

        return carry

    lax.fori_loop(0, n_row * n_col, greet, 0)

    def before(k, bound):
        total = jnp.int32(0)
        for l in range(n_list):
            total += jnp.where(lists[k, l] < bound, 1, 0).astype(jnp.int32)
        return total

    def first(begin, slots):
        return jnp.minimum(begin, n_list - slots)

    cur[slots_c] = jnp.zeros((width, width), cur.dtype)
    tot[slots_r] = jnp.zeros((width, width), tot.dtype)
    mine = first(before(r, col_base), slots_c)
    load_panel.wait()
    got[r] = panel[pl.ds(mine, slots_c)]
    pl.semaphore_wait(barrier, n_row * n_col - 1)

    chunk = slots_c // CHUNKS

    def go(k, q, step, sems):
        piece = got.at[k, pl.ds(q * chunk, chunk)]
        return pltpu.make_async_remote_copy(
            piece, piece, sems.at[k, q], x_r.at[k, q],
            device_id={"row": r + step}, device_id_type=MESH)

    def go_up(k, q):
        return go(k, q, 1, up_s)

    def go_down(k, q):
        return go(k, q, -1, down_s)

    def send_rows(k):
        return pltpu.make_async_remote_copy(
            got.at[k], quadx.at[k % k_col], qx_s.at[k], qx_r.at[k % k_col],
            device_id={"col": k // k_col}, device_id_type=MESH)

    def send_to_sibling(k, h):
        return pltpu.make_async_remote_copy(
            stage.at[k], sib_in.at[k], st_s.at[k], sib_r.at[k],
            device_id={"col": sibling}, device_id_type=MESH)

    def send_sum(k, target, which):
        return pltpu.make_async_remote_copy(
            x_stage.at[k], dest_x.at[k, chip, core], xs_s.at[k, which], dx_r.at[k, chip, core],
            device_id={"col": target}, device_id_type=MESH)

    def take_sum(k, q, h):
        return pltpu.make_async_remote_copy(
            x_stage.at[k], dest_x.at[k, q, h], xs_s.at[k, 0], dx_r.at[k, q, h],
            device_id={"col": q * 2 + h}, device_id_type=MESH)

    def share(k, target):
        return pltpu.make_async_remote_copy(
            quad_out.at[k], quad_in.at[r, k % k_col], q_s.at[k, target], q_r.at[r, k % k_col],
            device_id={"row": target, "col": k // k_col}, device_id_type=MESH)

    def take_share(at, other):
        return pltpu.make_async_remote_copy(
            quad_out.at[0], quad_in.at[other, at], q_s.at[0, 0], q_r.at[other, at],
            device_id={"row": other}, device_id_type=MESH)

    def crosses(k):
        return (k // k_col) // 2 != c_src // 2

    def lends_rows(k):
        return (c == c_src) & (k // k_col == sibling)

    def has_quad(k):
        return (crosses(k) & (c == c_src)) | (jnp.logical_not(crosses(k)) & (k // k_col == c))

    def pass_on(k, q):
        @pl.when(k != r)
        def _():
            go_up(k, q).wait_recv()

        @pl.when((k <= r) & (r < n_row - 1))
        def _():
            go_up(k, q).start()

        @pl.when((k >= r) & (r > 0))
        def _():
            go_down(k, q).start()

    def use(k):
        owner = k // k_col

        @pl.when(lends_rows(k))
        def _():
            send_rows(k).start()

        begin = before(k, col_base)
        base = first(begin, slots_c)
        cur[0:slots_c] = got[k]
        p = begin
        for j in range(cols_here):
            hit = lists[k, jnp.minimum(p, n_list - 1)] == col_base + j
            slot = jnp.where(hit, jnp.clip(p - base, 0, slots_c - 1), slots_c)
            xs[j * width : (j + 1) * width, :] = cur[slot]
            p += hit.astype(jnp.int32)

        @pl.when(k == r)
        def _():
            load_inv.wait()

        row_first = first(before(k, row_base), slots_r)

        def half_step(turn, carry):
            h = (core + 1 + turn) % 2
            lines = []
            for s in range(half):
                i = jnp.clip(lists[k, row_first + h * half + s] - row_base, 0, rows_here - 1)
                blocks = inv[i]
                lines.append(jnp.concatenate([blocks[j] for j in range(cols_here)], axis=1))
            left = jnp.concatenate(lines, axis=0)
            part[...] = jnp.dot(left, xs[...], preferred_element_type=jnp.float32)

            @pl.when(turn == 0)
            def _():
                stage[k] = part[...].astype(stage.dtype)
                send_to_sibling(k, h).start()

            @pl.when(turn == 1)
            def _():
                send_to_sibling(k, h).wait_recv()
                acc[k] = part[...] + sib_in[k].astype(jnp.float32)
                x_stage[k] = acc[k].astype(x_stage.dtype)

                @pl.when(owner != c)
                def _():
                    send_sum(k, owner, 0).start()

                @pl.when(crosses(k) & (c != c_src))
                def _():
                    send_sum(k, c_src, 1).start()

            return carry

        lax.fori_loop(0, 2, half_step, 0)

    def finish(k):
        owner = k // k_col
        at = k % k_col

        def gather_half(h, carry):
            def from_chip(q, carry):
                @pl.when((q != chip) | (h != core))
                def _():
                    take_sum(k, q, h).wait_recv()
                    come = dest_x[k, q, h].astype(jnp.float32).reshape(half, width, width)
                    where = pl.ds(h * half, half)

                    @pl.when(q == 0)
                    def _():
                        tot[where] = come

                    @pl.when(q > 0)
                    def _():
                        tot[where] = tot[where] + come

                @pl.when((q == chip) & (h == core))
                def _():
                    come = acc[k].reshape(half, width, width)
                    where = pl.ds(h * half, half)

                    @pl.when(q == 0)
                    def _():
                        tot[where] = come

                    @pl.when(q > 0)
                    def _():
                        tot[where] = tot[where] + come

                return carry

            return lax.fori_loop(0, n_chip, from_chip, carry)

        lax.fori_loop(0, 2, gather_half, 0)
        begin = before(k, row_base)
        row_first = first(begin, slots_r)

        @pl.when(has_quad(k))
        def _():
            col_first = first(before(k, c_src * cols_here), slots_c)

            @pl.when(c == c_src)
            def _():
                cur[0:slots_c] = got[k]

            @pl.when(c != c_src)
            def _():
                send_rows(k).wait_recv()
                cur[0:slots_c] = quadx[at]

            lines = []
            for s in range(slots_r):
                position = row_first + s
                number = lists[k, position] - row_base
                valid = (number >= 0) & (number < rows_here)
                slot = jnp.where(valid, jnp.clip(position - col_first, 0, slots_c - 1), slots_c)
                lines.append(cur[slot])
            left = jnp.concatenate(lines, axis=0)
            right = tot[0:slots_r].reshape(slots_r * width, width)
            high = right.astype(jnp.bfloat16)
            low = (right - high.astype(jnp.float32)).astype(jnp.bfloat16)
            both = lax.dot_general(
                left, jnp.concatenate([high, low], axis=1), (((0,), (0,)), ((), ())),
                preferred_element_type=jnp.float32)
            quad_out[k] = (both[:, :width] + both[:, width:]).astype(quad_out.dtype)

            def start_share(other, carry):
                @pl.when((other != r) | (owner != c))
                def _():
                    share(k, other).start()

                return carry

            lax.fori_loop(0, n_row, start_share, 0)

            @pl.when(owner == c)
            def _():
                quad_in[r, at] = quad_out[k]

        @pl.when(owner == c)
        def _():
            p = begin
            for i in range(rows_here):
                hit = lists[k, jnp.minimum(p, n_list - 1)] == row_base + i
                slot = jnp.where(hit, jnp.clip(p - row_first, 0, slots_r - 1), slots_r)
                off[at, i] = (-tot[slot]).astype(off.dtype)
                p += hit.astype(jnp.int32)

    def inside(k):
        return (k >= 0) & (k < n_row)

    def step(s, carry):
        def each(lap, body):
            k = r + jnp.where(lap == 0, -s, s)

            @pl.when(inside(k) & ((s > 0) | (lap == 0)))
            def _():
                body(k)

        def pass_step(i, carry):
            each(i % 2, lambda k: pass_on(k, i // 2))
            return carry

        lax.fori_loop(0, 2 * CHUNKS, pass_step, 0)

        def use_step(lap, carry):
            each(lap, use)
            return carry

        lax.fori_loop(0, 2, use_step, 0)

        def finish_step(lap, carry):
            last = s - 1
            k = r + jnp.where(lap == 0, -last, last)

            @pl.when(inside(k) & ((last > 0) | ((last == 0) & (lap == 0))))
            def _():
                owner = k // k_col

                @pl.when((owner == c) | (crosses(k) & (c == c_src)))
                def _():
                    finish(k)

            return carry

        lax.fori_loop(0, 2, finish_step, 0)
        return carry

    lax.fori_loop(0, n_row + 1, step, 0)

    def drain(k, carry):
        owner = k // k_col
        for q in range(CHUNKS):
            @pl.when((k <= r) & (r < n_row - 1))
            def _():
                go_up(k, q).wait_send()

            @pl.when((k >= r) & (r > 0))
            def _():
                go_down(k, q).wait_send()

        @pl.when(lends_rows(k))
        def _():
            send_rows(k).wait_send()

        send_to_sibling(k, 0).wait_send()

        @pl.when(owner != c)
        def _():
            send_sum(k, owner, 0).wait_send()

        @pl.when(crosses(k) & (c != c_src))
        def _():
            send_sum(k, c_src, 1).wait_send()

        @pl.when(has_quad(k))
        def _():
            def wait_share(other, carry):
                @pl.when((other != r) | (owner != c))
                def _():
                    share(k, other).wait_send()

                return carry

            lax.fori_loop(0, n_row, wait_share, 0)

        return carry

    lax.fori_loop(0, n_row, drain, 0)

    def arrive(at, carry):
        def one(other, carry):
            k = c * k_col + at

            @pl.when((other != r) | crosses(k))
            def _():
                take_share(at, other).wait_recv()

            return carry

        return lax.fori_loop(0, n_row, one, carry)

    lax.fori_loop(0, k_col, arrive, 0)

    quad = quad_in[0].astype(jnp.float32)
    for other in range(1, n_row):
        quad = quad + quad_in[other].astype(jnp.float32)
    diag[...] = dinv[...] + quad


def per_device(n_row, n_col, inverse_blocks, panel, lists, diag_inverse):
    rows_here, cols_here, width, _ = inverse_blocks.shape
    n_list = panel.shape[1]
    k_col = diag_inverse.shape[0]
    slots_r = slot_count(rows_here, n_list)
    slots_c = slot_count(cols_here, n_list)
    half = slots_r // 2
    n_super = n_row
    low, full = inverse_blocks.dtype, jnp.float32
    part = (half * width, width)
    dma = pltpu.SemaphoreType.DMA
    vmem = pl.BlockSpec(memory_space=pltpu.VMEM)
    return pl.pallas_call(
        functools.partial(
            kernel, n_row, n_col, k_col, rows_here, cols_here, n_list, slots_r, slots_c),
        out_shape=(
            jax.ShapeDtypeStruct((k_col, rows_here, width, width), low),
            jax.ShapeDtypeStruct((k_col, width, width), full),
        ),
        in_specs=[
            pl.BlockSpec(memory_space=pltpu.SMEM),
            pl.BlockSpec(memory_space=pl.ANY),
            pl.BlockSpec(memory_space=pl.ANY),
            vmem,
        ],
        out_specs=(vmem, vmem),
        scratch_shapes=[
            pltpu.VMEM(inverse_blocks.shape, low),
            pltpu.VMEM(panel.shape[1:], low),
            pltpu.VMEM((n_super, slots_c, width, width), low),
            pltpu.VMEM((slots_c + 1, width, width), low),
            pltpu.VMEM((cols_here * width, width), low),
            pltpu.VMEM(part, full),
            pltpu.VMEM((n_super,) + part, full),
            pltpu.VMEM((n_super,) + part, low),
            pltpu.VMEM((n_super,) + part, low),
            pltpu.VMEM((n_super,) + part, low),
            pltpu.VMEM((n_super, n_col // 2, 2) + part, low),
            pltpu.VMEM((k_col, slots_c, width, width), low),
            pltpu.VMEM((slots_r + 1, width, width), full),
            pltpu.VMEM((n_super, width, width), low),
            pltpu.VMEM((n_row, k_col, width, width), low),
            dma((2,)),
            dma((n_super, CHUNKS)),
            dma((n_super, CHUNKS)),
            dma((n_super, CHUNKS)),
            dma((n_super,)),
            dma((k_col,)),
            dma((n_super,)),
            dma((n_super,)),
            dma((n_super, 2)),
            dma((n_super, n_col // 2, 2)),
            dma((n_super, n_row)),
            dma((n_row, k_col)),
        ],
        compiler_params=pltpu.CompilerParams(
            collective_id=0, has_side_effects=True, vmem_limit_bytes=60 * 1024 * 1024),
        name="selected_inverse",
    )(lists, inverse_blocks, panel, diag_inverse)


def solution(mesh):
    in_specs = (
        P(("pole", "row"), "col", None, None),
        P(("pole", "row"), None, None, None),
        P(),
        P(("pole", "col"), None, None),
    )
    out_specs = (P(("pole", "col"), "row", None, None), P(("pole", "col"), None, None))
    return jax.shard_map(
        functools.partial(per_device, mesh.shape["row"], mesh.shape["col"]),
        mesh=mesh, in_specs=in_specs, out_specs=out_specs, check_vma=False)
```

time: 53.4 us -> 54.4 us (1.019)
  Pallas kernels: 48 us -> 50.1 us
  local copies, waits for them, and re-layouts: 4.16 us -> 3.36 us
    pallas_call x1, Pallas kernels: 48 us -> 50.1 us  [per_device(): pl.pallas_call(functools.partial(kernel, n_row, n_col, k_col, rows_here,...]
    unnamed x8 -> x2, local copies, waits for them, and re-layouts: 4.16 us -> 3.36 us
where the time goes in v2:
time: 54.4 us; the launch traced here: 54.1 us
  Pallas kernels  50.1 us (92%)
  local copies, waits for them, and re-layouts  3.36 us (6%)
  between operations  0.64 us (1%)
    pallas_call x1, Pallas kernels, per_device(): pl.pallas_call(functools.partial(kernel, n_row, n_col, k_col, rows_here,...  50.1 us
    unnamed x2, local copies, waits for them, and re-layouts  3.36 us

profile of v2, /device:TPU:0, one launch (start us, length us, event | category | flops | bytes accessed | tf_op | source)
XLA Modules:
  0.0 54.1 jit_solution(12262241347875431048)
XLA Ops:
  0.6 50.1 %selected_inverse.1 = (bf16[1,16,128,128]{3,2,1,0:T(8,128)(2,1)}, f32[1,128,128]{2,1,0:T(8,128)}) custom-call(s32[4,32]{1,0:T(4,128)} %lists.1, bf16[16,16,128,128]{3,2,1,0:T(8,128)(2,1)} %inv_hbm.1, bf16[1,32,128,128]{3,2,1,0:T(8,128)(2,1)} %panel_hbm.1, f32[1,128,128]{2,1,0:T(8,128)} %dinv.1), custom_call_target="tpu_custom_call" | custom-call | tf_op jit(solution)/shard_map/selected_inverse/pallas_call | solution.py:403
  50.8 1.9 %copy.8 = bf16[1,16,128,128]{3,2,1,0:T(8,128)(2,1)} copy(bf16[1,16,128,128]{3,2,1,0:T(8,128)(2,1)} %get-tuple-element.4) | data formatting | bytes 1048576
  52.7 1.5 %copy.9 = f32[1,128,128]{2,1,0:T(8,128)} copy(f32[1,128,128]{2,1,0:T(8,128)} %get-tuple-element.5) | data formatting | bytes 131072

commit v3 on v2

--- a/solution.py
+++ b/solution.py
@@ -25,8 +25,8 @@
 
 def kernel(
     n_row, n_col, k_col, rows_here, cols_here, n_list, slots_r, slots_c,
-    lists, inv_hbm, panel_hbm, dinv, off, diag,
-    inv, panel, got, cur, xs, part, acc, stage, x_stage, sib_in, dest_x,
+    lists_hbm, inv_hbm, panel_hbm, off, diag,
+    lists, inv, panel, got, cur, xs, part, acc, stage, x_stage, sib_in, dest_x,
     quadx, tot, quad_out, quad_in,
     load_sem, up_s, down_s, x_r, qx_s, qx_r, st_s, sib_r, xs_s, dx_r, q_s, q_r,
 ):
@@ -42,8 +42,9 @@
 
     load_panel = pltpu.make_async_copy(panel_hbm.at[0], panel, load_sem.at[0])
     load_inv = pltpu.make_async_copy(inv_hbm, inv, load_sem.at[1])
+    load_lists = pltpu.make_async_copy(lists_hbm, lists, load_sem.at[2])
+    load_lists.start()
     load_panel.start()
-    load_inv.start()
 
     barrier = pltpu.get_barrier_semaphore()
     def greet(at, carry):
@@ -65,13 +66,15 @@
     def first(begin, slots):
         return jnp.minimum(begin, n_list - slots)
 
+    load_lists.wait()
+    mine = first(before(r, col_base), slots_c)
+    load_panel.wait()
+    load_inv.start()
+    got[r] = panel[pl.ds(mine, slots_c)]
+    pl.semaphore_wait(barrier, n_row * n_col - 1)
+
     cur[slots_c] = jnp.zeros((width, width), cur.dtype)
     tot[slots_r] = jnp.zeros((width, width), tot.dtype)
-    mine = first(before(r, col_base), slots_c)
-    load_panel.wait()
-    got[r] = panel[pl.ds(mine, slots_c)]
-    pl.semaphore_wait(barrier, n_row * n_col - 1)
-
     chunk = slots_c // CHUNKS
 
     def go(k, q, step, sems):
@@ -301,14 +304,12 @@
             each(i % 2, lambda k: pass_on(k, i // 2))
             return carry
 
-        lax.fori_loop(0, 2 * CHUNKS, pass_step, 0)
+        lax.fori_loop(0, 2 * CHUNKS - 2, pass_step, 0)
 
         def use_step(lap, carry):
             each(lap, use)
             return carry
 
-        lax.fori_loop(0, 2, use_step, 0)
-
         def finish_step(lap, carry):
             last = s - 1
             k = r + jnp.where(lap == 0, -last, last)
@@ -324,6 +325,8 @@
             return carry
 
         lax.fori_loop(0, 2, finish_step, 0)
+        lax.fori_loop(2 * CHUNKS - 2, 2 * CHUNKS, pass_step, 0)
+        lax.fori_loop(0, 2, use_step, 0)
         return carry
 
     lax.fori_loop(0, n_row + 1, step, 0)
@@ -385,7 +388,23 @@
     quad = quad_in[0].astype(jnp.float32)
     for other in range(1, n_row):
         quad = quad + quad_in[other].astype(jnp.float32)
-    diag[...] = dinv[...] + quad
+    diag[...] = quad
+
+
+def close(product, quad, dinv, off, diag, update, base, sems):
+    keep = pltpu.make_async_copy(product, off, sems.at[0])
+    load_update = pltpu.make_async_copy(quad, update, sems.at[1])
+    load_base = pltpu.make_async_copy(dinv, base, sems.at[2])
+    keep.start()
+    load_update.start()
+    load_base.start()
+    load_update.wait()
+    load_base.wait()
+    update[...] = base[...] + update[...]
+    store = pltpu.make_async_copy(update, diag, sems.at[3])
+    store.start()
+    keep.wait()
+    store.wait()
 
 
 def per_device(n_row, n_col, inverse_blocks, panel, lists, diag_inverse):
@@ -400,21 +419,19 @@
     part = (half * width, width)
     dma = pltpu.SemaphoreType.DMA
     vmem = pl.BlockSpec(memory_space=pltpu.VMEM)
-    return pl.pallas_call(
+    hbm = pl.BlockSpec(memory_space=pltpu.HBM)
+    anywhere = pl.BlockSpec(memory_space=pl.ANY)
+    product, quad = pl.pallas_call(
         functools.partial(
             kernel, n_row, n_col, k_col, rows_here, cols_here, n_list, slots_r, slots_c),
         out_shape=(
             jax.ShapeDtypeStruct((k_col, rows_here, width, width), low),
             jax.ShapeDtypeStruct((k_col, width, width), full),
         ),
-        in_specs=[
-            pl.BlockSpec(memory_space=pltpu.SMEM),
-            pl.BlockSpec(memory_space=pl.ANY),
-            pl.BlockSpec(memory_space=pl.ANY),
-            vmem,
-        ],
+        in_specs=[hbm] * 3,
         out_specs=(vmem, vmem),
         scratch_shapes=[
+            pltpu.SMEM(lists.shape, lists.dtype),
             pltpu.VMEM(inverse_blocks.shape, low),
             pltpu.VMEM(panel.shape[1:], low),
             pltpu.VMEM((n_super, slots_c, width, width), low),
@@ -430,7 +447,7 @@
             pltpu.VMEM((slots_r + 1, width, width), full),
             pltpu.VMEM((n_super, width, width), low),
             pltpu.VMEM((n_row, k_col, width, width), low),
-            dma((2,)),
+            dma((3,)),
             dma((n_super, CHUNKS)),
             dma((n_super, CHUNKS)),
             dma((n_super, CHUNKS)),
@@ -444,9 +461,25 @@
             dma((n_row, k_col)),
         ],
         compiler_params=pltpu.CompilerParams(
-            collective_id=0, has_side_effects=True, vmem_limit_bytes=60 * 1024 * 1024),
+            collective_id=0, has_side_effects=True, vmem_limit_bytes=53760 * 1024),
         name="selected_inverse",
-    )(lists, inverse_blocks, panel, diag_inverse)
+    )(lists, inverse_blocks, panel)
+    return pl.pallas_call(
+        close,
+        out_shape=(
+            jax.ShapeDtypeStruct(product.shape, low),
+            jax.ShapeDtypeStruct(quad.shape, full),
+        ),
+        in_specs=[anywhere] * 3,
+        out_specs=(anywhere, anywhere),
+        scratch_shapes=[
+            pltpu.VMEM(quad.shape, full),
+            pltpu.VMEM(quad.shape, full),
+            dma((4,)),
+        ],
+        compiler_params=pltpu.CompilerParams(vmem_limit_bytes=4 * 1024 * 1024),
+        name="close",
+    )(product, quad, diag_inverse)
 
 
 def solution(mesh):

time: 54.4 us -> 51.5 us (0.947)
  local copies, waits for them, and re-layouts: 3.36 us -> 0.71 us
    unnamed x2 -> x4, local copies, waits for them, and re-layouts: 3.36 us -> 0.71 us
    pallas_call x1, Pallas kernels: 50.1 us -> 49.1 us  [per_device(): pl.pallas_call(functools.partial(kernel, n_row, n_col, k_col, rows_here,...]
    pallas_call x0 -> x1, Pallas kernels: none -> 0.85 us  [per_device(): pl.pallas_call(close, out_shape=(jax.ShapeDtypeStruct(product.shape, low)...]
where the time goes in v3:
time: 51.5 us; the launch traced here: 51.3 us
  Pallas kernels  49.9 us (97%)
  local copies, waits for them, and re-layouts  0.71 us (1%)
  between operations  0.66 us (1%)
    pallas_call x1, Pallas kernels, per_device(): pl.pallas_call(functools.partial(kernel, n_row, n_col, k_col, rows_here,...  49.1 us

profile of v3, /device:TPU:0, one launch (start us, length us, event | category | flops | bytes accessed | tf_op | source)
XLA Modules:
  0.0 51.3 jit_solution(14090576399955009470)
XLA Ops:
  0.6 0.0 copy-start
  0.6 0.0 copy-start.1
  0.7 0.7 %copy-done.1 = s32[4,32]{1,0:T(4,128)S(1)} copy-done((s32[4,32]{1,0:T(4,128)S(1)}, s32[4,32]{1,0:T(4,128)}, u32[]{:S(2)}) %copy-start.1) | copy-done | bytes 536
  1.4 49.1 %selected_inverse.1 = (bf16[1,16,128,128]{3,2,1,0:T(8,128)(2,1)S(1)}, f32[1,128,128]{2,1,0:T(8,128)S(1)}) custom-call(s32[4,32]{1,0:T(4,128)S(1)} %copy-done.1, bf16[16,16,128,128]{3,2,1,0:T(8,128)(2,1)} %inv_hbm.1, bf16[1,32,128,128]{3,2,1,0:T(8,128)(2,1)} %panel_hbm.1), custom_call_target="tpu_custom_call" | custom-call | tf_op jit(solution)/shard_map/selected_inverse/pallas_call | solution.py:424
  50.4 0.0 copy-done
  50.4 0.8 %close.1 = (bf16[1,16,128,128]{3,2,1,0:T(8,128)(2,1)}, f32[1,128,128]{2,1,0:T(8,128)}) custom-call(bf16[1,16,128,128]{3,2,1,0:T(8,128)(2,1)S(1)} %get-tuple-element.4.product, f32[1,128,128]{2,1,0:T(8,128)S(1)} %get-tuple-element.5.quad, f32[1,128,128]{2,1,0:T(8,128)S(1)} %copy-done), custom_call_target="tpu_custom_call" | custom-call | tf_op jit(solution)/shard_map/close/pallas_call | solution.py:467
Async XLA Ops:
  0.6 49.8 %copy-start = (f32[1,128,128]{2,1,0:T(8,128)S(1)}, f32[1,128,128]{2,1,0:T(8,128)}, u32[]{:S(2)}) copy-start(f32[1,128,128]{2,1,0:T(8,128)} %dinv.1) | copy-start | bytes 196612
  0.6 0.7 %copy-start.1 = (s32[4,32]{1,0:T(4,128)S(1)}, s32[4,32]{1,0:T(4,128)}, u32[]{:S(2)}) copy-start(s32[4,32]{1,0:T(4,128)} %lists_hbm.1) | copy-start | bytes 1540

commit v4 on v3

--- a/solution.py
+++ b/solution.py
@@ -24,7 +24,7 @@
 
 
 def kernel(
-    n_row, n_col, k_col, rows_here, cols_here, n_list, slots_r, slots_c,
+    n_row, n_col, k_col, rows_here, cols_here, n_list, slots_r, slots_c, pieces,
     lists_hbm, inv_hbm, panel_hbm, off, diag,
     lists, inv, panel, got, cur, xs, part, acc, stage, x_stage, sib_in, dest_x,
     quadx, tot, quad_out, quad_in,
@@ -36,6 +36,7 @@
     chip, core = c // 2, c % 2
     sibling = chip * 2 + 1 - core
     half = slots_r // 2
+    piece = half // pieces
     n_chip = n_col // 2
     row_base, col_base = r * rows_here, c * cols_here
     c_src = row_base // cols_here
@@ -94,19 +95,20 @@
             got.at[k], quadx.at[k % k_col], qx_s.at[k], qx_r.at[k % k_col],
             device_id={"col": k // k_col}, device_id_type=MESH)
 
-    def send_to_sibling(k, h):
-        return pltpu.make_async_remote_copy(
-            stage.at[k], sib_in.at[k], st_s.at[k], sib_r.at[k],
+    def send_to_sibling(k, w):
+        return pltpu.make_async_remote_copy(
+            stage.at[k, w], sib_in.at[k, w], st_s.at[k, w], sib_r.at[k, w],
             device_id={"col": sibling}, device_id_type=MESH)
 
-    def send_sum(k, target, which):
-        return pltpu.make_async_remote_copy(
-            x_stage.at[k], dest_x.at[k, chip, core], xs_s.at[k, which], dx_r.at[k, chip, core],
+    def send_sum(k, target, which, w):
+        return pltpu.make_async_remote_copy(
+            x_stage.at[k, w], dest_x.at[k, chip, core, w], xs_s.at[k, which, w],
+            dx_r.at[k, chip, core, w],
             device_id={"col": target}, device_id_type=MESH)
 
-    def take_sum(k, q, h):
-        return pltpu.make_async_remote_copy(
-            x_stage.at[k], dest_x.at[k, q, h], xs_s.at[k, 0], dx_r.at[k, q, h],
+    def take_sum(k, q, h, w):
+        return pltpu.make_async_remote_copy(
+            x_stage.at[k, w], dest_x.at[k, q, h, w], xs_s.at[k, 0, w], dx_r.at[k, q, h, w],
             device_id={"col": q * 2 + h}, device_id_type=MESH)
 
     def share(k, target):
@@ -165,49 +167,52 @@
         row_first = first(before(k, row_base), slots_r)
 
         def half_step(turn, carry):
-            h = (core + 1 + turn) % 2
+            h = (core + 1 + turn // pieces) % 2
+            w = turn % pieces
             lines = []
-            for s in range(half):
-                i = jnp.clip(lists[k, row_first + h * half + s] - row_base, 0, rows_here - 1)
+            for s in range(piece):
+                i = jnp.clip(lists[k, row_first + h * half + w * piece + s] - row_base, 0, rows_here - 1)
                 blocks = inv[i]
                 lines.append(jnp.concatenate([blocks[j] for j in range(cols_here)], axis=1))
             left = jnp.concatenate(lines, axis=0)
             part[...] = jnp.dot(left, xs[...], preferred_element_type=jnp.float32)
 
-            @pl.when(turn == 0)
-            def _():
-                stage[k] = part[...].astype(stage.dtype)
-                send_to_sibling(k, h).start()
-
-            @pl.when(turn == 1)
-            def _():
-                send_to_sibling(k, h).wait_recv()
-                acc[k] = part[...] + sib_in[k].astype(jnp.float32)
-                x_stage[k] = acc[k].astype(x_stage.dtype)
+            @pl.when(turn < pieces)
+            def _():
+                stage[k, w] = part[...].astype(stage.dtype)
+                send_to_sibling(k, w).start()
+
+            @pl.when(turn >= pieces)
+            def _():
+                send_to_sibling(k, w).wait_recv()
+                acc[k, w] = part[...] + sib_in[k, w].astype(jnp.float32)
+                x_stage[k, w] = acc[k, w].astype(x_stage.dtype)
 
                 @pl.when(owner != c)
                 def _():
-                    send_sum(k, owner, 0).start()
+                    send_sum(k, owner, 0, w).start()
 
                 @pl.when(crosses(k) & (c != c_src))
                 def _():
-                    send_sum(k, c_src, 1).start()
+                    send_sum(k, c_src, 1, w).start()
 
             return carry
 
-        lax.fori_loop(0, 2, half_step, 0)
+        lax.fori_loop(0, 2 * pieces, half_step, 0)
 
     def finish(k):
         owner = k // k_col
         at = k % k_col
 
-        def gather_half(h, carry):
+        def gather_piece(part_at, carry):
+            h, w = part_at % 2, part_at // 2
+
             def from_chip(q, carry):
                 @pl.when((q != chip) | (h != core))
                 def _():
-                    take_sum(k, q, h).wait_recv()
-                    come = dest_x[k, q, h].astype(jnp.float32).reshape(half, width, width)
-                    where = pl.ds(h * half, half)
+                    take_sum(k, q, h, w).wait_recv()
+                    come = dest_x[k, q, h, w].astype(jnp.float32).reshape(piece, width, width)
+                    where = pl.ds(h * half + w * piece, piece)
 
                     @pl.when(q == 0)
                     def _():
@@ -219,8 +224,8 @@
 
                 @pl.when((q == chip) & (h == core))
                 def _():
-                    come = acc[k].reshape(half, width, width)
-                    where = pl.ds(h * half, half)
+                    come = acc[k, w].reshape(piece, width, width)
+                    where = pl.ds(h * half + w * piece, piece)
 
                     @pl.when(q == 0)
                     def _():
@@ -234,7 +239,7 @@
 
             return lax.fori_loop(0, n_chip, from_chip, carry)
 
-        lax.fori_loop(0, 2, gather_half, 0)
+        lax.fori_loop(0, 2 * pieces, gather_piece, 0)
         begin = before(k, row_base)
         row_first = first(begin, slots_r)
 
@@ -346,15 +351,16 @@
         def _():
             send_rows(k).wait_send()
 
-        send_to_sibling(k, 0).wait_send()
-
-        @pl.when(owner != c)
-        def _():
-            send_sum(k, owner, 0).wait_send()
-
-        @pl.when(crosses(k) & (c != c_src))
-        def _():
-            send_sum(k, c_src, 1).wait_send()
+        for w in range(pieces):
+            send_to_sibling(k, w).wait_send()
+
+            @pl.when(owner != c)
+            def _():
+                send_sum(k, owner, 0, w).wait_send()
+
+            @pl.when(crosses(k) & (c != c_src))
+            def _():
+                send_sum(k, c_src, 1, w).wait_send()
 
         @pl.when(has_quad(k))
         def _():
@@ -416,14 +422,15 @@
     half = slots_r // 2
     n_super = n_row
     low, full = inverse_blocks.dtype, jnp.float32
-    part = (half * width, width)
+    pieces = 2 if half % 2 == 0 else 1
+    part = (half // pieces * width, width)
     dma = pltpu.SemaphoreType.DMA
     vmem = pl.BlockSpec(memory_space=pltpu.VMEM)
     hbm = pl.BlockSpec(memory_space=pltpu.HBM)
     anywhere = pl.BlockSpec(memory_space=pl.ANY)
     product, quad = pl.pallas_call(
         functools.partial(
-            kernel, n_row, n_col, k_col, rows_here, cols_here, n_list, slots_r, slots_c),
+            kernel, n_row, n_col, k_col, rows_here, cols_here, n_list, slots_r, slots_c, pieces),
         out_shape=(
             jax.ShapeDtypeStruct((k_col, rows_here, width, width), low),
             jax.ShapeDtypeStruct((k_col, width, width), full),
@@ -438,11 +445,11 @@
             pltpu.VMEM((slots_c + 1, width, width), low),
             pltpu.VMEM((cols_here * width, width), low),
             pltpu.VMEM(part, full),
-            pltpu.VMEM((n_super,) + part, full),
-            pltpu.VMEM((n_super,) + part, low),
-            pltpu.VMEM((n_super,) + part, low),
-            pltpu.VMEM((n_super,) + part, low),
-            pltpu.VMEM((n_super, n_col // 2, 2) + part, low),
+            pltpu.VMEM((n_super, pieces) + part, full),
+            pltpu.VMEM((n_super, pieces) + part, low),
+            pltpu.VMEM((n_super, pieces) + part, low),
+            pltpu.VMEM((n_super, pieces) + part, low),
+            pltpu.VMEM((n_super, n_col // 2, 2, pieces) + part, low),
             pltpu.VMEM((k_col, slots_c, width, width), low),
             pltpu.VMEM((slots_r + 1, width, width), full),
             pltpu.VMEM((n_super, width, width), low),
@@ -453,10 +460,10 @@
             dma((n_super, CHUNKS)),
             dma((n_super,)),
             dma((k_col,)),
-            dma((n_super,)),
-            dma((n_super,)),
-            dma((n_super, 2)),
-            dma((n_super, n_col // 2, 2)),
+            dma((n_super, pieces)),
+            dma((n_super, pieces)),
+            dma((n_super, 2, pieces)),
+            dma((n_super, n_col // 2, 2, pieces)),
             dma((n_super, n_row)),
             dma((n_row, k_col)),
         ],

time: 51.5 us -> 50.6 us (0.983)
  Pallas kernels: 49.9 us -> 49 us
    pallas_call x1, Pallas kernels: 49.1 us -> 48.2 us  [per_device(): pl.pallas_call(functools.partial(kernel, n_row, n_col, k_col, rows_here,...]
where the time goes in v4:
time: 50.6 us; the launch traced here: 50.4 us
  Pallas kernels  49 us (97%)
  local copies, waits for them, and re-layouts  0.71 us (1%)
  between operations  0.66 us (1%)
    pallas_call x1, Pallas kernels, per_device(): pl.pallas_call(functools.partial(kernel, n_row, n_col, k_col, rows_here,...  48.2 us

profile of v4, /device:TPU:0, one launch (start us, length us, event | category | flops | bytes accessed | tf_op | source)
XLA Modules:
  0.0 50.4 jit_solution(11253397633157272072)
XLA Ops:
  0.6 0.0 copy-start
  0.6 0.0 copy-start.1
  0.7 0.7 %copy-done.1 = s32[4,32]{1,0:T(4,128)S(1)} copy-done((s32[4,32]{1,0:T(4,128)S(1)}, s32[4,32]{1,0:T(4,128)}, u32[]{:S(2)}) %copy-start.1) | copy-done | bytes 536
  1.4 48.2 %selected_inverse.1 = (bf16[1,16,128,128]{3,2,1,0:T(8,128)(2,1)S(1)}, f32[1,128,128]{2,1,0:T(8,128)S(1)}) custom-call(s32[4,32]{1,0:T(4,128)S(1)} %copy-done.1, bf16[16,16,128,128]{3,2,1,0:T(8,128)(2,1)} %inv_hbm.1, bf16[1,32,128,128]{3,2,1,0:T(8,128)(2,1)} %panel_hbm.1), custom_call_target="tpu_custom_call" | custom-call | tf_op jit(solution)/shard_map/selected_inverse/pallas_call | solution.py:431
  49.5 0.0 copy-done
  49.5 0.8 %close.1 = (bf16[1,16,128,128]{3,2,1,0:T(8,128)(2,1)}, f32[1,128,128]{2,1,0:T(8,128)}) custom-call(bf16[1,16,128,128]{3,2,1,0:T(8,128)(2,1)S(1)} %get-tuple-element.4.product, f32[1,128,128]{2,1,0:T(8,128)S(1)} %get-tuple-element.5.quad, f32[1,128,128]{2,1,0:T(8,128)S(1)} %copy-done), custom_call_target="tpu_custom_call" | custom-call | tf_op jit(solution)/shard_map/close/pallas_call | solution.py:474
Async XLA Ops:
  0.6 48.9 %copy-start = (f32[1,128,128]{2,1,0:T(8,128)S(1)}, f32[1,128,128]{2,1,0:T(8,128)}, u32[]{:S(2)}) copy-start(f32[1,128,128]{2,1,0:T(8,128)} %dinv.1) | copy-start | bytes 196612
  0.6 0.7 %copy-start.1 = (s32[4,32]{1,0:T(4,128)S(1)}, s32[4,32]{1,0:T(4,128)}, u32[]{:S(2)}) copy-start(s32[4,32]{1,0:T(4,128)} %lists_hbm.1) | copy-start | bytes 1540

commit v5 on v4

--- a/solution.py
+++ b/solution.py
@@ -153,12 +153,12 @@
         begin = before(k, col_base)
         base = first(begin, slots_c)
         cur[0:slots_c] = got[k]
-        p = begin
-        for j in range(cols_here):
-            hit = lists[k, jnp.minimum(p, n_list - 1)] == col_base + j
-            slot = jnp.where(hit, jnp.clip(p - base, 0, slots_c - 1), slots_c)
-            xs[j * width : (j + 1) * width, :] = cur[slot]
-            p += hit.astype(jnp.int32)
+        columns = []
+        for t in range(slots_c):
+            number = lists[k, base + t] - col_base
+            valid = (number >= 0) & (number < cols_here)
+            xs[t * width : (t + 1) * width, :] = cur[jnp.where(valid, t, slots_c)]
+            columns.append(jnp.clip(number, 0, cols_here - 1))
 
         @pl.when(k == r)
         def _():
@@ -172,8 +172,7 @@
             lines = []
             for s in range(piece):
                 i = jnp.clip(lists[k, row_first + h * half + w * piece + s] - row_base, 0, rows_here - 1)
-                blocks = inv[i]
-                lines.append(jnp.concatenate([blocks[j] for j in range(cols_here)], axis=1))
+                lines.append(jnp.concatenate([inv[i, j] for j in columns], axis=1))
             left = jnp.concatenate(lines, axis=0)
             part[...] = jnp.dot(left, xs[...], preferred_element_type=jnp.float32)
 
@@ -443,7 +442,7 @@
             pltpu.VMEM(panel.shape[1:], low),
             pltpu.VMEM((n_super, slots_c, width, width), low),
             pltpu.VMEM((slots_c + 1, width, width), low),
-            pltpu.VMEM((cols_here * width, width), low),
+            pltpu.VMEM((slots_c * width, width), low),
             pltpu.VMEM(part, full),
             pltpu.VMEM((n_super, pieces) + part, full),
             pltpu.VMEM((n_super, pieces) + part, low),

time: 50.6 us -> 50.4 us (level)
  no operation moved by 1% of the time
where the time goes in v5:
time: 50.4 us; the launch traced here: 50.2 us
  Pallas kernels  48.8 us (97%)
  local copies, waits for them, and re-layouts  0.71 us (1%)
  between operations  0.66 us (1%)
    pallas_call x1, Pallas kernels, per_device(): pl.pallas_call(functools.partial(kernel, n_row, n_col, k_col, rows_here,...  48 us

profile of v5, /device:TPU:0, one launch (start us, length us, event | category | flops | bytes accessed | tf_op | source)
XLA Modules:
  0.0 50.2 jit_solution(14435697340292564966)
XLA Ops:
  0.6 0.0 copy-start
  0.6 0.0 copy-start.1
  0.7 0.7 %copy-done.1 = s32[4,32]{1,0:T(4,128)S(1)} copy-done((s32[4,32]{1,0:T(4,128)S(1)}, s32[4,32]{1,0:T(4,128)}, u32[]{:S(2)}) %copy-start.1) | copy-done | bytes 536
  1.4 48.0 %selected_inverse.1 = (bf16[1,16,128,128]{3,2,1,0:T(8,128)(2,1)S(1)}, f32[1,128,128]{2,1,0:T(8,128)S(1)}) custom-call(s32[4,32]{1,0:T(4,128)S(1)} %copy-done.1, bf16[16,16,128,128]{3,2,1,0:T(8,128)(2,1)} %inv_hbm.1, bf16[1,32,128,128]{3,2,1,0:T(8,128)(2,1)} %panel_hbm.1), custom_call_target="tpu_custom_call" | custom-call | tf_op jit(solution)/shard_map/selected_inverse/pallas_call | solution.py:430
  49.3 0.0 copy-done
  49.3 0.8 %close.1 = (bf16[1,16,128,128]{3,2,1,0:T(8,128)(2,1)}, f32[1,128,128]{2,1,0:T(8,128)}) custom-call(bf16[1,16,128,128]{3,2,1,0:T(8,128)(2,1)S(1)} %get-tuple-element.4.product, f32[1,128,128]{2,1,0:T(8,128)S(1)} %get-tuple-element.5.quad, f32[1,128,128]{2,1,0:T(8,128)S(1)} %copy-done), custom_call_target="tpu_custom_call" | custom-call | tf_op jit(solution)/shard_map/close/pallas_call | solution.py:473
Async XLA Ops:
  0.6 48.7 %copy-start = (f32[1,128,128]{2,1,0:T(8,128)S(1)}, f32[1,128,128]{2,1,0:T(8,128)}, u32[]{:S(2)}) copy-start(f32[1,128,128]{2,1,0:T(8,128)} %dinv.1) | copy-start | bytes 196612
  0.6 0.7 %copy-start.1 = (s32[4,32]{1,0:T(4,128)S(1)}, s32[4,32]{1,0:T(4,128)}, u32[]{:S(2)}) copy-start(s32[4,32]{1,0:T(4,128)} %lists_hbm.1) | copy-start | bytes 1540
